TPU v7x, 128 devices: a whole 4x4x4 slice. The times are simulated.
128 devices in a mesh: row: 16 (over z_lo, x, core), col: 8 (over z_hi, y).
Axes of the slice: x: 4, y: 4, z: 4 (z_hi: 2, z_lo: 2; z = z_hi * 2 + z_lo), core: 2. Of those that a mesh axis runs over, the one named last changes fastest.
Arguments:
- features: bfloat16 [65536, 256], P(('row', 'col')), may hold values from -6 to 6
- tile_edge_weights: bfloat16 [16, 8, 736, 128, 128], P('row', 'col'), as said below
- slot_block_row: int32 [16, 8, 736], P('row', 'col'), may hold values from 0 to 32, as said below
- slot_block_column: int32 [16, 8, 736], P('row', 'col'), may hold values from 0 to 63, as said below
- degree: int32 [65536], P(('row', 'col')), may hold values from 14 to 56
- w_self: bfloat16 [256, 256], replicated, may hold values from -0.375 to 0.375
- w_neigh: bfloat16 [256, 256], replicated, may hold values from -0.375 to 0.375
Outputs:
- updated: bfloat16 [65536, 256], P(('row', 'col'))
Inputs may be any that keep to these rules, and one draw needn't show every extreme that they name: `slot_block_row`: block slot rows: live slots come first in each tile; dead slots hold 4 * 8. Each tile has between 184 and 736 live slots, distinct (row, column) pairs; some tile is full and some tile has 184. `slot_block_column`: dead slots hold the largest column. `tile_edge_weights`: each block holds about 40 nonzero edge weights, the rest zero.
All inputs are finite; a program needn't handle non-finite values.
Results may differ from a plain program's by a relative error of at most 0.0034.
Values may be sent and summed in bfloat16 or wider, within the bound.
A program may use at most 128 MiB of HBM per device.

v0:
```python
import jax
import jax.numpy as jnp
from jax import lax
from jax.sharding import PartitionSpec as P


def add_group(acc, slot_ids, valid, row_indices, column_indices, entry_values, source, first_blk):
    out_blocks = acc.shape[0]
    block_extent = entry_values.shape[-1]
    width = source.shape[-1]
    src_blocks = source.shape[0] // block_extent
    blocks = source.reshape(src_blocks, block_extent, width)
    row_ids = row_indices[slot_ids]
    local = jnp.clip(column_indices[slot_ids] - first_blk, 0, src_blocks - 1)
    picked = blocks[local]
    prod = jnp.einsum(
        "sij,sjd->sid", entry_values[slot_ids], picked, preferred_element_type=jnp.float32
    )
    keep = valid & (row_ids < out_blocks)
    target = jnp.where(keep, row_ids, out_blocks)
    return acc.at[target].add(prod, mode="drop")


def per_device(
    features, tile_edge_weights, slot_block_row, slot_block_column, degree, w_self, w_neigh
):
    width = features.shape[1]
    block_extent = tile_edge_weights.shape[-1]
    slot_count = tile_edge_weights.shape[2]
    entry_values = tile_edge_weights.reshape(slot_count, block_extent, block_extent)
    row_indices = slot_block_row.reshape(slot_count)
    column_indices = slot_block_column.reshape(slot_count)
    out_blocks = lax.axis_size("col") * (features.shape[0] // block_extent)
    live = jnp.sum((row_indices < out_blocks).astype(jnp.int32))
    lanes = jnp.arange(32, dtype=jnp.int32)
    empty = jnp.zeros((out_blocks, block_extent, width), jnp.float32)
    gathered = lax.all_gather(features, "row", axis=0, tiled=True)

    def step_whole(g, acc):
        slot_ids = g * 32 + lanes
        return add_group(
            acc, slot_ids, slot_ids < live, row_indices, column_indices, entry_values, gathered, 0
        )

    total = lax.fori_loop(0, (live + 31) // 32, step_whole, empty)
    terms = total.reshape(out_blocks * block_extent, width)
    summed = lax.psum_scatter(terms, "col", scatter_dimension=0, tiled=True)
    neighbour_mean = (summed / degree.astype(jnp.float32)[:, None]).astype(jnp.bfloat16)
    own = jnp.dot(features, w_self, preferred_element_type=jnp.float32)
    other = jnp.dot(neighbour_mean, w_neigh, preferred_element_type=jnp.float32)
    return jax.nn.relu(own + other).astype(jnp.bfloat16)


def solution(mesh):
    in_specs = (
        P(("row", "col"), None),
        P("row", "col", None, None, None),
        P("row", "col", None),
        P("row", "col", None),
        P(("row", "col")),
        P(),
        P(),
    )
    out_specs = P(("row", "col"), None)
    return jax.shard_map(
        per_device, mesh=mesh, in_specs=in_specs, out_specs=out_specs, check_vma=False
    )
```

profile of v0, /device:TPU:0, one launch (start us, length us, event | category | flops | bytes accessed | tf_op | source)
XLA Modules:
  0.0 746.0 jit_solution(8411521256750491457)
XLA Ops:
  10.0 39.0 %all-gather.2.cloned.1.call-done = bf16[8192,256]{1,0:T(8,128)(2,1)} async-done(((bf16[512,256]{1,0:T(8,128)(2,1)}), bf16[8192,256]{1,0:T(8,128)(2,1)}) %all-gather.2.cloned.1.call-update) | async-done | bytes 4194320 | tf_op jit(solution)/shard_map/all_gather | solution.py:37
  51.5 287.0 %while.11 = (s32[]{:T(128)}, f32[32,128,256]{2,1,0:T(8,128)}, s32[]{:T(128)}, s32[]{:T(128)}, s32[736]{0:T(1024)S(1)}, /*index=5*/bf16[736,128,128]{2,1,0:T(8,12...) while((s32[]{:T(128)}, f32[32,128,256]{2,1,0:T(8,128)}, s32[]{:T(128)}, ...), condition=%wide.region_3.4_spmd.clone, body=%wide.region_1.3_spmd.clone.sunk | while | flops 269486592 | bytes 26224764 | solution.py:45
  52.2 2.9 gather_fusion.3
  55.1 8.6 %gather_fusion.1 = bf16[32,128,128]{2,1,0:T(8,128)(2,1)S(1)} fusion(bf16[736,128,128]{2,1,0:T(8,128)(2,1)} %get-tuple-element.164, s32[1024]{0:T(1024)S(1)} %pad_clamp_fusion.4), kind=kCustom, calls=%fused_computation.1.clone.clone.1 | custom fusion | bytes 2097280 | tf_op jit(solution)/shard_map/while/body/gather | solution.py:17
  67.7 9.8 %scatter_fusion = f32[32,128,256]{2,1,0:T(8,128)} fusion(f32[32,128,256]{2,1,0:T(8,128)} %get-tuple-element.150, s32[32]{0:T(128)S(1)} %fusion.24, f32[32,128,256]{2,1,0:T(8,128)} %fusion.26), kind=kCustom, calls=%fused_computation.4.clone.clone.1 | custom fusion | flops 1048576 | bytes 12583040 | tf_op jit(solution)/shard_map/while/body/scatter-add | solution.py:21
  78.3 2.9 gather_fusion.3
  81.1 8.6 %gather_fusion.1 = bf16[32,128,128]{2,1,0:T(8,128)(2,1)S(1)} fusion(bf16[736,128,128]{2,1,0:T(8,128)(2,1)} %get-tuple-element.164, s32[1024]{0:T(1024)S(1)} %pad_clamp_fusion.4), kind=kCustom, calls=%fused_computation.1.clone.clone.1 | custom fusion | bytes 2097280 | tf_op jit(solution)/shard_map/while/body/gather | solution.py:17
  93.8 9.8 %scatter_fusion = f32[32,128,256]{2,1,0:T(8,128)} fusion(f32[32,128,256]{2,1,0:T(8,128)} %get-tuple-element.150, s32[32]{0:T(128)S(1)} %fusion.24, f32[32,128,256]{2,1,0:T(8,128)} %fusion.26), kind=kCustom, calls=%fused_computation.4.clone.clone.1 | custom fusion | flops 1048576 | bytes 12583040 | tf_op jit(solution)/shard_map/while/body/scatter-add | solution.py:21
  104.3 2.9 gather_fusion.3
  107.1 8.6 %gather_fusion.1 = bf16[32,128,128]{2,1,0:T(8,128)(2,1)S(1)} fusion(bf16[736,128,128]{2,1,0:T(8,128)(2,1)} %get-tuple-element.164, s32[1024]{0:T(1024)S(1)} %pad_clamp_fusion.4), kind=kCustom, calls=%fused_computation.1.clone.clone.1 | custom fusion | bytes 2097280 | tf_op jit(solution)/shard_map/while/body/gather | solution.py:17
  119.8 9.9 %scatter_fusion = f32[32,128,256]{2,1,0:T(8,128)} fusion(f32[32,128,256]{2,1,0:T(8,128)} %get-tuple-element.150, s32[32]{0:T(128)S(1)} %fusion.24, f32[32,128,256]{2,1,0:T(8,128)} %fusion.26), kind=kCustom, calls=%fused_computation.4.clone.clone.1 | custom fusion | flops 1048576 | bytes 12583040 | tf_op jit(solution)/shard_map/while/body/scatter-add | solution.py:21
  130.4 2.9 gather_fusion.3
  133.3 8.6 %gather_fusion.1 = bf16[32,128,128]{2,1,0:T(8,128)(2,1)S(1)} fusion(bf16[736,128,128]{2,1,0:T(8,128)(2,1)} %get-tuple-element.164, s32[1024]{0:T(1024)S(1)} %pad_clamp_fusion.4), kind=kCustom, calls=%fused_computation.1.clone.clone.1 | custom fusion | bytes 2097280 | tf_op jit(solution)/shard_map/while/body/gather | solution.py:17
  145.9 9.9 %scatter_fusion = f32[32,128,256]{2,1,0:T(8,128)} fusion(f32[32,128,256]{2,1,0:T(8,128)} %get-tuple-element.150, s32[32]{0:T(128)S(1)} %fusion.24, f32[32,128,256]{2,1,0:T(8,128)} %fusion.26), kind=kCustom, calls=%fused_computation.4.clone.clone.1 | custom fusion | flops 1048576 | bytes 12583040 | tf_op jit(solution)/shard_map/while/body/scatter-add | solution.py:21
  156.5 2.9 gather_fusion.3
  159.3 8.6 %gather_fusion.1 = bf16[32,128,128]{2,1,0:T(8,128)(2,1)S(1)} fusion(bf16[736,128,128]{2,1,0:T(8,128)(2,1)} %get-tuple-element.164, s32[1024]{0:T(1024)S(1)} %pad_clamp_fusion.4), kind=kCustom, calls=%fused_computation.1.clone.clone.1 | custom fusion | bytes 2097280 | tf_op jit(solution)/shard_map/while/body/gather | solution.py:17
  172.0 9.9 %scatter_fusion = f32[32,128,256]{2,1,0:T(8,128)} fusion(f32[32,128,256]{2,1,0:T(8,128)} %get-tuple-element.150, s32[32]{0:T(128)S(1)} %fusion.24, f32[32,128,256]{2,1,0:T(8,128)} %fusion.26), kind=kCustom, calls=%fused_computation.4.clone.clone.1 | custom fusion | flops 1048576 | bytes 12583040 | tf_op jit(solution)/shard_map/while/body/scatter-add | solution.py:21
  182.5 2.9 gather_fusion.3
  185.4 8.6 %gather_fusion.1 = bf16[32,128,128]{2,1,0:T(8,128)(2,1)S(1)} fusion(bf16[736,128,128]{2,1,0:T(8,128)(2,1)} %get-tuple-element.164, s32[1024]{0:T(1024)S(1)} %pad_clamp_fusion.4), kind=kCustom, calls=%fused_computation.1.clone.clone.1 | custom fusion | bytes 2097280 | tf_op jit(solution)/shard_map/while/body/gather | solution.py:17
  198.0 9.9 %scatter_fusion = f32[32,128,256]{2,1,0:T(8,128)} fusion(f32[32,128,256]{2,1,0:T(8,128)} %get-tuple-element.150, s32[32]{0:T(128)S(1)} %fusion.24, f32[32,128,256]{2,1,0:T(8,128)} %fusion.26), kind=kCustom, calls=%fused_computation.4.clone.clone.1 | custom fusion | flops 1048576 | bytes 12583040 | tf_op jit(solution)/shard_map/while/body/scatter-add | solution.py:21
  211.5 8.6 %gather_fusion.1 = bf16[32,128,128]{2,1,0:T(8,128)(2,1)S(1)} fusion(bf16[736,128,128]{2,1,0:T(8,128)(2,1)} %get-tuple-element.164, s32[1024]{0:T(1024)S(1)} %pad_clamp_fusion.4), kind=kCustom, calls=%fused_computation.1.clone.clone.1 | custom fusion | bytes 2097280 | tf_op jit(solution)/shard_map/while/body/gather | solution.py:17
  224.1 9.9 %scatter_fusion = f32[32,128,256]{2,1,0:T(8,128)} fusion(f32[32,128,256]{2,1,0:T(8,128)} %get-tuple-element.150, s32[32]{0:T(128)S(1)} %fusion.24, f32[32,128,256]{2,1,0:T(8,128)} %fusion.26), kind=kCustom, calls=%fused_computation.4.clone.clone.1 | custom fusion | flops 1048576 | bytes 12583040 | tf_op jit(solution)/shard_map/while/body/scatter-add | solution.py:21
  237.6 8.6 %gather_fusion.1 = bf16[32,128,128]{2,1,0:T(8,128)(2,1)S(1)} fusion(bf16[736,128,128]{2,1,0:T(8,128)(2,1)} %get-tuple-element.164, s32[1024]{0:T(1024)S(1)} %pad_clamp_fusion.4), kind=kCustom, calls=%fused_computation.1.clone.clone.1 | custom fusion | bytes 2097280 | tf_op jit(solution)/shard_map/while/body/gather | solution.py:17
  250.2 9.9 %scatter_fusion = f32[32,128,256]{2,1,0:T(8,128)} fusion(f32[32,128,256]{2,1,0:T(8,128)} %get-tuple-element.150, s32[32]{0:T(128)S(1)} %fusion.24, f32[32,128,256]{2,1,0:T(8,128)} %fusion.26), kind=kCustom, calls=%fused_computation.4.clone.clone.1 | custom fusion | flops 1048576 | bytes 12583040 | tf_op jit(solution)/shard_map/while/body/scatter-add | solution.py:21
  260.8 2.9 gather_fusion.3
  263.7 8.6 %gather_fusion.1 = bf16[32,128,128]{2,1,0:T(8,128)(2,1)S(1)} fusion(bf16[736,128,128]{2,1,0:T(8,128)(2,1)} %get-tuple-element.164, s32[1024]{0:T(1024)S(1)} %pad_clamp_fusion.4), kind=kCustom, calls=%fused_computation.1.clone.clone.1 | custom fusion | bytes 2097280 | tf_op jit(solution)/shard_map/while/body/gather | solution.py:17
  276.3 10.0 %scatter_fusion = f32[32,128,256]{2,1,0:T(8,128)} fusion(f32[32,128,256]{2,1,0:T(8,128)} %get-tuple-element.150, s32[32]{0:T(128)S(1)} %fusion.24, f32[32,128,256]{2,1,0:T(8,128)} %fusion.26), kind=kCustom, calls=%fused_computation.4.clone.clone.1 | custom fusion | flops 1048576 | bytes 12583040 | tf_op jit(solution)/shard_map/while/body/scatter-add | solution.py:21
  289.8 8.6 %gather_fusion.1 = bf16[32,128,128]{2,1,0:T(8,128)(2,1)S(1)} fusion(bf16[736,128,128]{2,1,0:T(8,128)(2,1)} %get-tuple-element.164, s32[1024]{0:T(1024)S(1)} %pad_clamp_fusion.4), kind=kCustom, calls=%fused_computation.1.clone.clone.1 | custom fusion | bytes 2097280 | tf_op jit(solution)/shard_map/while/body/gather | solution.py:17
  302.4 10.1 %scatter_fusion = f32[32,128,256]{2,1,0:T(8,128)} fusion(f32[32,128,256]{2,1,0:T(8,128)} %get-tuple-element.150, s32[32]{0:T(128)S(1)} %fusion.24, f32[32,128,256]{2,1,0:T(8,128)} %fusion.26), kind=kCustom, calls=%fused_computation.4.clone.clone.1 | custom fusion | flops 1048576 | bytes 12583040 | tf_op jit(solution)/shard_map/while/body/scatter-add | solution.py:21
  316.1 8.6 %gather_fusion.1 = bf16[32,128,128]{2,1,0:T(8,128)(2,1)S(1)} fusion(bf16[736,128,128]{2,1,0:T(8,128)(2,1)} %get-tuple-element.164, s32[1024]{0:T(1024)S(1)} %pad_clamp_fusion.4), kind=kCustom, calls=%fused_computation.1.clone.clone.1 | custom fusion | bytes 2097280 | tf_op jit(solution)/shard_map/while/body/gather | solution.py:17
  328.7 9.8 %scatter_fusion = f32[32,128,256]{2,1,0:T(8,128)} fusion(f32[32,128,256]{2,1,0:T(8,128)} %get-tuple-element.150, s32[32]{0:T(128)S(1)} %fusion.24, f32[32,128,256]{2,1,0:T(8,128)} %fusion.26), kind=kCustom, calls=%fused_computation.4.clone.clone.1 | custom fusion | flops 1048576 | bytes 12583040 | tf_op jit(solution)/shard_map/while/body/scatter-add | solution.py:21
  339.7 397.4 %reduce-scatter.2.cloned.1.call-done = f32[512,256]{1,0:T(8,128)} async-done(((f32[4096,256]{1,0:T(8,128)}), f32[512,256]{1,0:T(8,128)}) %reduce-scatter.2.cloned.1.call-update) | async-done | bytes 524304 | tf_op jit(solution)/shard_map/reduce_scatter | solution.py:47
  (111 shorter events, 71.1 us)
Async XLA Ops:
  6.5 332.6 %copy-start = (bf16[256,256]{1,0:T(8,128)(2,1)S(1)}, bf16[256,256]{1,0:T(8,128)(2,1)}, u32[]{:S(2)}) copy-start(bf16[256,256]{1,0:T(8,128)(2,1)} %param.14) | copy-start | bytes 393220
  6.5 42.5 %all-gather.2.cloned.1.call-start = ((), (), s32[]{:S(2)}) async-start(), calls=%async_computation.1 | async-start | bytes 4456448 | tf_op jit(solution)/shard_map/all_gather | solution.py:37
  7.3 729.9 %reduce-scatter.2.cloned.1.call-start = ((), (), s32[]{:S(2)}) async-start(), calls=%async_computation.2 | async-start | bytes 4718592 | tf_op jit(solution)/shard_map/reduce_scatter | solution.py:47
  338.5 0.7 copy-start.2
  338.5 1.0 copy-start.1
  338.5 398.6 %copy-start.3 = (bf16[256,256]{1,0:T(8,128)(2,1)S(1)}, bf16[256,256]{1,0:T(8,128)(2,1)}, u32[]{:S(2)}) copy-start(bf16[256,256]{1,0:T(8,128)(2,1)} %param.15) | copy-start | bytes 393220
Sparse Core Ops, SparseCore 0:
  9.1 39.9 all-gather.1
  338.7 398.4 reduce-scatter.1
where the time goes:
time: 749 us; the launch traced here: 746 us
  waiting for transfers between devices  437 us (58%)
  local copies, waits for them, and re-layouts  145 us (19%)
  other arithmetic  118 us (16%)
  matrix products  31.6 us (4%)
  between operations  14.1 us (2%)
    reduce_scatter x1, waiting for transfers between devices, per_device(): summed = lax.psum_scatter(terms, 'col', scatter_dimension=0, tiled=True)  397 us
    scatter-add x11, other arithmetic, add_group(): return acc.at[target].add(prod, mode='drop')  109 us
    gather x11, local copies, waits for them, and re-layouts, add_group(): entry_values[slot_ids]  95.1 us
    all_gather x1, waiting for transfers between devices, per_device(): gathered = lax.all_gather(features, 'row', axis=0, tiled=True)  39 us
    gather x11, local copies, waits for them, and re-layouts, add_group(): picked = blocks[local]  31.6 us
    dot_general x11, matrix products, add_group(): jnp.einsum('sij,sjd->sid', entry_values[slot_ids], picked, preferred_elem...  29.3 us
  transfers between devices with their start and end apart: 2, of which 2 were waited for; matrix products, arithmetic and copies ran while one was open for 0% of the time, Pallas kernels for 0%

commit v1 on v0

v1 whole, which is shorter than its diff:
```python
import functools

import jax
import jax.numpy as jnp
from jax import lax
from jax.experimental import pallas as pl
from jax.experimental.pallas import tpu as pltpu
from jax.sharding import PartitionSpec as P

MESH = pl.DeviceIdType.MESH
BS = 128
D = 256
PIECE = 512
NBLK = 736
LANES = 768
ROW_BLOCKS = 32
COL_BLOCKS = 64
CHUNK = 16


def row_at(i, dz, dx, dc):
    return ((i // 8 + dz) % 2) * 8 + ((i // 2 + dx + 4) % 4) * 2 + (i + dc) % 2


def col_at(j, dz, dy):
    return ((j // 4 + dz) % 2) * 4 + (j + dy + 4) % 4


def gather_plan():
    half, quarter = PIECE // 2, PIECE // 4
    upper, lower = (0, half), (half, half)
    right, left, over, core = (0, 1, 0), (0, -1, 0), (1, 0, 0), (0, 0, 1)
    return [
        (None, [
            ("a1", (0, 0), *upper, right), ("a2", (0, 0), *upper, left),
            ("bz", (0, 0), *lower, over), ("az", (0, 0), *upper, over),
            ("b1", (0, 0), *lower, right), ("b2", (0, 0), *lower, left),
            ("s0", (0, 0), 0, PIECE, core)]),
        ("a1", [("az1", (0, -1), *upper, over), ("a3", (0, -1), 0, quarter, right),
                ("s1", (0, -1), *upper, core)]),
        ("a2", [("az2", (0, 1), *upper, over), ("a4", (0, 1), quarter, quarter, left),
                ("s2", (0, 1), *upper, core)]),
        ("bz", [("zb1", (1, 0), *lower, right), ("zb2", (1, 0), *lower, left),
                ("s3", (1, 0), *lower, core)]),
        ("b1", [("b3", (0, -1), half, quarter, right), ("s4", (0, -1), *lower, core)]),
        ("b2", [("b4", (0, 1), half + quarter, quarter, left), ("s5", (0, 1), *lower, core)]),
        ("az", [("s6", (1, 0), *upper, core)]),
        ("a3", [("az3", (0, 2), 0, quarter, over), ("s7", (0, 2), 0, quarter, core)]),
        ("a4", [("az4", (0, 2), quarter, quarter, over), ("s8", (0, 2), quarter, quarter, core)]),
        ("zb1", [("zb3", (1, -1), half, quarter, right), ("s9", (1, -1), *lower, core)]),
        ("zb2", [("zb4", (1, 1), half + quarter, quarter, left), ("s10", (1, 1), *lower, core)]),
        ("az1", [("s11", (1, -1), *upper, core)]),
        ("az2", [("s12", (1, 1), *upper, core)]),
        ("b3", [("s13", (0, 2), half, quarter, core)]),
        ("b4", [("s14", (0, 2), half + quarter, quarter, core)]),
        ("zb3", [("s15", (1, 2), half, quarter, core)]),
        ("zb4", [("s16", (1, 2), half + quarter, quarter, core)]),
        ("az3", [("s17", (1, 2), 0, quarter, core)]),
        ("az4", [("s18", (1, 2), quarter, quarter, core)]),
    ]


PLAN = gather_plan()
SENDS = {copy[0]: copy for _, copies in PLAN for copy in copies}
PLACE = {name: k for k, name in enumerate(SENDS)}


def step_offset(k):
    m = k // 2
    return 1 - k % 2, (2 + m + m * (m - 1) // 2) % 4


def kernel(
    rows_ref, cols_ref, degree_ref, w_self_ref, w_neigh_ref, x_hbm, a_hbm, out_ref,
    gathered, blocks, table_v, table_s, own, acc, sent, got, slots,
    load_sem, x_sem, table_sem, g_send, g_recv, c_send, c_recv,
):
    i, j = lax.axis_index("row"), lax.axis_index("col")

    load = pltpu.make_async_copy(a_hbm, blocks.at[pl.ds(1, NBLK)], load_sem)
    load.start()
    x_load = pltpu.make_async_copy(x_hbm, gathered.at[i], x_sem)
    x_load.start()

    barrier = pltpu.get_barrier_semaphore()
    near = [(0, 1, 0), (0, -1, 0), (1, 0, 0), (0, 0, 1)]
    for offset in near:
        pl.semaphore_signal(barrier, inc=1, device_id=(row_at(i, *offset), j), device_id_type=MESH)
    for k in range(7):
        pl.semaphore_signal(
            barrier, inc=1, device_id=(i, col_at(j, *step_offset(k))), device_id_type=MESH)
    pl.semaphore_wait(barrier, len(near) + 7)

    def gather_copy(name, arriving=False):
        _, (dz, dx), first, count, target = SENDS[name]
        if arriving:
            place = row_at(i, dz - target[0], dx - target[1], -target[2])
        else:
            place = row_at(i, dz, dx, 0)
        region = gathered.at[place, pl.ds(first, count)]
        source = region
        if not arriving and (dz, dx) == (0, 0):
            source = x_hbm.at[pl.ds(first, count)]
        return pltpu.make_async_remote_copy(
            src_ref=source, dst_ref=region,
            send_sem=g_send.at[PLACE[name]], recv_sem=g_recv.at[PLACE[name]],
            device_id=(row_at(i, *target), j), device_id_type=MESH)

    waited = set()

    def gather_steps(steps):
        for name, copies in steps:
            if name is not None:
                gather_copy(name, arriving=True).wait_recv()
                waited.add(name)
            for copy in copies:
                gather_copy(copy[0]).start()

    gather_steps(PLAN[:1])

    slots[...] = jnp.full_like(slots, -1)
    slots[0:1, 0:NBLK] = rows_ref[...]
    slots[1:2, 0:NBLK] = cols_ref[...]
    place = lax.broadcasted_iota(jnp.int32, (COL_BLOCKS, LANES), 1) + 1
    here = lax.broadcasted_iota(jnp.int32, (COL_BLOCKS, LANES), 0) == slots[1:2, :]
    in_row = lax.broadcasted_iota(jnp.int32, (ROW_BLOCKS, LANES), 0) == slots[0:1, :]
    in_row = in_row.astype(jnp.float32).astype(jnp.bfloat16)
    high = jnp.where(here, place >> 5, 0).astype(jnp.float32).astype(jnp.bfloat16)
    low = jnp.where(here, place & 31, 0).astype(jnp.float32).astype(jnp.bfloat16)
    dims = (((1,), (1,)), ((), ()))
    found = 32.0 * lax.dot_general(in_row, high, dims, preferred_element_type=jnp.float32)
    found += lax.dot_general(in_row, low, dims, preferred_element_type=jnp.float32)
    table_v[...] = jnp.clip(found.astype(jnp.int32), 0, NBLK)
    table_copy = pltpu.make_async_copy(table_v, table_s, table_sem)
    table_copy.start()
    blocks[0] = jnp.zeros((BS, BS), jnp.bfloat16)

    gather_steps(PLAN[1:3])
    x_load.wait()
    gather_steps(PLAN[3:4])
    for b in range(4):
        rows = pl.ds(b * BS, BS)
        own[rows, :] = jnp.dot(
            gathered[i, rows, :], w_self_ref[...], preferred_element_type=jnp.float32)
    gather_steps(PLAN[4:])
    table_copy.wait()
    for name in SENDS:
        if name not in waited:
            gather_copy(name, arriving=True).wait_recv()
    load.wait()

    def piece_sum(piece):
        acc[...] = jnp.zeros_like(acc)

        def chunk(c, _):
            for p in range(0, CHUNK, 2):
                first = c * CHUNK + p
                block = first % 4
                x = gathered[first // 4, pl.ds(pl.multiple_of(block * BS, 2 * BS), 2 * BS), :]
                for b in range(4):
                    r = piece * 4 + b
                    a = jnp.concatenate(
                        [blocks[table_s[r, first]], blocks[table_s[r, first + 1]]], axis=1)
                    acc[b] += jnp.dot(a, x, preferred_element_type=jnp.float32)
            return 0

        lax.fori_loop(0, COL_BLOCKS // CHUNK, chunk, 0)

    def piece_copy(k):
        return pltpu.make_async_remote_copy(
            src_ref=sent.at[k], dst_ref=got.at[k], send_sem=c_send.at[k], recv_sem=c_recv.at[k],
            device_id=(i, col_at(j, *step_offset(k))), device_id_type=MESH)

    def send_step(k, _):
        piece_sum(col_at(j, *step_offset(k)))
        for b in range(4):
            sent[k, pl.ds(b * BS, BS), :] = acc[b].astype(jnp.bfloat16)
        piece_copy(k).start()
        return 0

    lax.fori_loop(0, 7, send_step, 0)
    piece_sum(j)
    for k in range(7):
        piece_copy(k).wait_recv()
    for b in range(4):
        rows = pl.ds(b * BS, BS)
        total = acc[b]
        for k in range(7):
            total += got[k, rows, :].astype(jnp.float32)
        degree = jnp.broadcast_to(degree_ref[b:b + 1, :].astype(jnp.float32), (BS, BS)).T
        degree = jnp.concatenate([degree, degree], axis=1)
        mean = (total / degree).astype(jnp.bfloat16)
        new = own[rows, :] + jnp.dot(mean, w_neigh_ref[...], preferred_element_type=jnp.float32)
        out_ref[rows, :] = jnp.maximum(new, 0.0).astype(jnp.bfloat16)
    for k in range(7):
        piece_copy(k).wait_send()
    for name in SENDS:
        gather_copy(name).wait_send()


def per_device(features, weights, slot_row, slot_column, degree, w_self, w_neigh):
    vmem = pl.BlockSpec(memory_space=pltpu.VMEM)
    hbm = pl.BlockSpec(memory_space=pl.ANY)
    count = len(SENDS)
    return pl.pallas_call(
        kernel,
        out_shape=jax.ShapeDtypeStruct((PIECE, D), jnp.bfloat16),
        in_specs=[vmem] * 5 + [hbm] * 2,
        out_specs=vmem,
        scratch_shapes=[
            pltpu.VMEM((16, PIECE, D), jnp.bfloat16),
            pltpu.VMEM((NBLK + 1, BS, BS), jnp.bfloat16),
            pltpu.VMEM((ROW_BLOCKS, COL_BLOCKS), jnp.int32),
            pltpu.SMEM((ROW_BLOCKS, COL_BLOCKS), jnp.int32),
            pltpu.VMEM((PIECE, D), jnp.float32),
            pltpu.VMEM((4, BS, D), jnp.float32),
            pltpu.VMEM((7, PIECE, D), jnp.bfloat16),
            pltpu.VMEM((7, PIECE, D), jnp.bfloat16),
            pltpu.VMEM((8, LANES), jnp.int32),
            pltpu.SemaphoreType.DMA,
            pltpu.SemaphoreType.DMA,
            pltpu.SemaphoreType.DMA,
            pltpu.SemaphoreType.DMA((count,)),
            pltpu.SemaphoreType.DMA((count,)),
            pltpu.SemaphoreType.DMA((7,)),
            pltpu.SemaphoreType.DMA((7,)),
        ],
        compiler_params=pltpu.CompilerParams(
            collective_id=0, has_side_effects=True, vmem_limit_bytes=52 * 2**20),
        name="sage_layer",
    )(
        slot_row.reshape(1, NBLK), slot_column.reshape(1, NBLK), degree.reshape(4, BS),
        w_self, w_neigh, features, weights.reshape(NBLK, BS, BS),
    )


def solution(mesh):
    in_specs = (
        P(("row", "col"), None),
        P("row", "col", None, None, None),
        P("row", "col", None),
        P("row", "col", None),
        P(("row", "col")),
        P(),
        P(),
    )
    return jax.shard_map(
        per_device, mesh=mesh, in_specs=in_specs, out_specs=P(("row", "col"), None), check_vma=False)
```

time: 749 us -> 65.1 us (0.09)
  waiting for transfers between devices: 437 us -> 0 us
  local copies, waits for them, and re-layouts: 145 us -> 5.51 us
  other arithmetic: 118 us -> 0 us
  Pallas kernels: 0 us -> 58.3 us
  matrix products: 31.6 us -> 0 us
  between operations: 14.1 us -> 0.02 us
    reduce_scatter x1 -> x0, waiting for transfers between devices: 397 us -> none  [per_device(): summed = lax.psum_scatter(terms, 'col', scatter_dimension=0, tiled=True)]
    gather x44 -> x0, local copies, waits for them, and re-layouts: 141 us -> none  [the longest x11 95.1 us: add_group(): entry_values[slot_ids]]
    scatter-add x11 -> x0, other arithmetic: 109 us -> none  [add_group(): return acc.at[target].add(prod, mode='drop')]
    pallas_call x0 -> x1, Pallas kernels: none -> 58.3 us  [per_device(): pl.pallas_call(kernel, out_shape=jax.ShapeDtypeStruct((PIECE, D), jnp.bfl...]
    all_gather x1 -> x0, waiting for transfers between devices: 39 us -> none  [per_device(): gathered = lax.all_gather(features, 'row', axis=0, tiled=True)]
    dot_general x13 -> x0, matrix products: 31.6 us -> none  [the longest x11 29.3 us: add_group(): jnp.einsum('sij,sjd->sid', entry_values[slot_ids], picked, preferred_elem...]
  transfers between devices with their start and end apart: 2 -> 0, of which waited for: 2 -> 0; matrix products, arithmetic and copies ran while one was open for 0% -> 0% of each run, Pallas kernels for 0% -> 0%
where the time goes in v1:
time: 65.1 us; the launch traced here: 63.8 us
  Pallas kernels  58.3 us (90%)
  local copies, waits for them, and re-layouts  5.51 us (8%)
    pallas_call x1, Pallas kernels, per_device(): pl.pallas_call(kernel, out_shape=jax.ShapeDtypeStruct((PIECE, D), jnp.bfl...  58.3 us
    unnamed x13, local copies, waits for them, and re-layouts  5.51 us

profile of v1, /device:TPU:0, one launch (start us, length us, event | category | flops | bytes accessed | tf_op | source)
XLA Modules:
  0.0 63.8 jit_solution(1817332695245923757)
XLA Ops:
  0.0 0.0 copy-start
  0.0 0.9 %copy-done = bf16[512,256]{1,0:T(8,128)(2,1)S(1)} copy-done((bf16[512,256]{1,0:T(8,128)(2,1)S(1)}, bf16[512,256]{1,0:T(8,128)(2,1)}, u32[]{:S(2)}) %copy-start) | copy-done | bytes 262168
  1.0 0.0 copy-start.1
  1.0 0.9 %copy-done.1 = bf16[256,256]{1,0:T(8,128)(2,1)S(1)} copy-done((bf16[256,256]{1,0:T(8,128)(2,1)S(1)}, bf16[256,256]{1,0:T(8,128)(2,1)}, u32[]{:S(2)}) %copy-start.1) | copy-done | bytes 131096
  1.9 0.0 copy-start.2
  1.9 0.9 %copy-done.2 = bf16[256,256]{1,0:T(8,128)(2,1)S(1)} copy-done((bf16[256,256]{1,0:T(8,128)(2,1)S(1)}, bf16[256,256]{1,0:T(8,128)(2,1)}, u32[]{:S(2)}) %copy-start.2) | copy-done | bytes 131096
  2.8 0.0 copy-start.3
  2.8 0.7 %copy-done.3 = s32[1,1,736]{2,1,0:T(1,128)S(1)} copy-done((s32[1,1,736]{2,1,0:T(1,128)S(1)}, s32[1,1,736]{2,1,0:T(1,128)}, u32[]{:S(2)}) %copy-start.3) | copy-done | bytes 2968
  3.4 0.0 copy-start.4
  3.4 0.7 %copy-done.4 = s32[1,1,736]{2,1,0:T(1,128)S(1)} copy-done((s32[1,1,736]{2,1,0:T(1,128)S(1)}, s32[1,1,736]{2,1,0:T(1,128)}, u32[]{:S(2)}) %copy-start.4) | copy-done | bytes 2968
  4.1 0.0 copy-start.5
  4.1 0.7 %copy-done.5 = s32[512]{0:T(512)S(1)} copy-done((s32[512]{0:T(512)S(1)}, s32[512]{0:T(512)}, u32[]{:S(2)}) %copy-start.5) | copy-done | bytes 2072
  4.8 58.3 %sage_layer.1 = bf16[512,256]{1,0:T(8,128)(2,1)S(1)} custom-call(s32[1,736]{1,0:T(1,128)S(1)} %bitcast.4, s32[1,736]{1,0:T(1,128)S(1)} %bitcast.5, s32[4,128]{1,0:T(4,128)S(1)} %bitcast.6, bf16[256,256]{1,0:T(8,128)(2,1)S(1)} %copy-done.1, bf16[256,256]{1,0:T(8,128)(2,1)S(1)} %copy-done.2, bf16[512,256]{1,0:T(8,128)(2,1)S(1)} %copy-done, ...), custom_call_target="tpu_custom_call" | custom-call | tf_op jit(solution)/shard_map/sage_layer/pallas_call | solution.py:205
  63.1 0.7 %copy.9 = bf16[512,256]{1,0:T(8,128)(2,1)} copy(bf16[512,256]{1,0:T(8,128)(2,1)S(1)} %sage_layer.1) | data formatting | bytes 524288
Async XLA Ops:
  0.0 0.9 %copy-start = (bf16[512,256]{1,0:T(8,128)(2,1)S(1)}, bf16[512,256]{1,0:T(8,128)(2,1)}, u32[]{:S(2)}) copy-start(bf16[512,256]{1,0:T(8,128)(2,1)} %x_hbm.1) | copy-start | bytes 786436
  1.0 0.9 %copy-start.1 = (bf16[256,256]{1,0:T(8,128)(2,1)S(1)}, bf16[256,256]{1,0:T(8,128)(2,1)}, u32[]{:S(2)}) copy-start(bf16[256,256]{1,0:T(8,128)(2,1)} %w_self_ref.1) | copy-start | bytes 393220
  1.9 0.9 %copy-start.2 = (bf16[256,256]{1,0:T(8,128)(2,1)S(1)}, bf16[256,256]{1,0:T(8,128)(2,1)}, u32[]{:S(2)}) copy-start(bf16[256,256]{1,0:T(8,128)(2,1)} %w_neigh_ref.1) | copy-start | bytes 393220
  2.8 0.7 %copy-start.3 = (s32[1,1,736]{2,1,0:T(1,128)S(1)}, s32[1,1,736]{2,1,0:T(1,128)}, u32[]{:S(2)}) copy-start(s32[1,1,736]{2,1,0:T(1,128)} %param.9) | copy-start | bytes 8836
  3.4 0.7 %copy-start.4 = (s32[1,1,736]{2,1,0:T(1,128)S(1)}, s32[1,1,736]{2,1,0:T(1,128)}, u32[]{:S(2)}) copy-start(s32[1,1,736]{2,1,0:T(1,128)} %param.10) | copy-start | bytes 8836
  4.1 0.7 %copy-start.5 = (s32[512]{0:T(512)S(1)}, s32[512]{0:T(512)}, u32[]{:S(2)}) copy-start(s32[512]{0:T(512)} %param.11) | copy-start | bytes 6148

commit v2 on v1

--- a/solution.py
+++ b/solution.py
@@ -1,5 +1,3 @@
-import functools
-
 import jax
 import jax.numpy as jnp
 from jax import lax
@@ -15,7 +13,6 @@
 LANES = 768
 ROW_BLOCKS = 32
 COL_BLOCKS = 64
-CHUNK = 16
 
 
 def row_at(i, dz, dx, dc):
@@ -65,31 +62,61 @@
 PLACE = {name: k for k, name in enumerate(SENDS)}
 
 
-def step_offset(k):
-    m = k // 2
-    return 1 - k % 2, (2 + m + m * (m - 1) // 2) % 4
+STEPS = [(1, 2), (1, -1), (1, 1), (0, 2), (1, 0), (0, -1), (0, 1), (0, 0)]
+EARLY = [(0, 0), (0, 1), (0, -1)]
+LATE = [(1, 0), (0, 2), (1, 1), (1, -1), (1, 2)]
+Z_ROWS = 256
+Y_HALF = Z_ROWS + (PIECE - Z_ROWS) // 2
+OVER, RIGHT, LEFT = (1, 0), (0, 1), (0, -1)
+PARTS = {
+    "z2": ((1, 2), 0, Z_ROWS, OVER), "zl": ((1, -1), 0, Z_ROWS, OVER),
+    "zr": ((1, 1), 0, Z_ROWS, OVER),
+    "o2r": ((1, 2), Z_ROWS, Y_HALF - Z_ROWS, RIGHT), "o2l": ((1, 2), Y_HALF, PIECE - Y_HALF, LEFT),
+    "o1r": ((1, 1), Z_ROWS, PIECE - Z_ROWS, RIGHT), "o1l": ((1, -1), Z_ROWS, PIECE - Z_ROWS, LEFT),
+    "n2r": ((0, 2), 0, PIECE // 2, RIGHT), "n2l": ((0, 2), PIECE // 2, PIECE // 2, LEFT),
+    "n1r": ((0, 1), 0, PIECE, RIGHT), "n1l": ((0, -1), 0, PIECE, LEFT),
+    "o0": ((1, 0), 0, PIECE, OVER),
+}
+PART_PLACE = {name: k for k, name in enumerate(PARTS)}
+PART_START = {}
+PART_ROWS = 0
+for _name, _part in PARTS.items():
+    PART_START[_name] = PART_ROWS
+    PART_ROWS += _part[2]
+
+
+def step_piece(j, k):
+    dz, dy = 0, 0
+    for step, (z, y) in enumerate(STEPS):
+        dz = jnp.where(k == step, z, dz)
+        dy = jnp.where(k == step, y, dy)
+    return col_at(j, dz, dy)
 
 
 def kernel(
-    rows_ref, cols_ref, degree_ref, w_self_ref, w_neigh_ref, x_hbm, a_hbm, out_ref,
+    rows_hbm, cols_hbm, degree_hbm, w_self_hbm, w_neigh_hbm, x_hbm, a_hbm, out_ref,
     gathered, blocks, table_v, table_s, own, acc, sent, got, slots,
-    load_sem, x_sem, table_sem, g_send, g_recv, c_send, c_recv,
+    rows_v, cols_v, degree_v, w_self, w_neigh,
+    load_sem, table_sem, g_send, g_recv, c_send, c_recv,
 ):
     i, j = lax.axis_index("row"), lax.axis_index("col")
 
-    load = pltpu.make_async_copy(a_hbm, blocks.at[pl.ds(1, NBLK)], load_sem)
-    load.start()
-    x_load = pltpu.make_async_copy(x_hbm, gathered.at[i], x_sem)
-    x_load.start()
+    loads = [
+        pltpu.make_async_copy(source, target, load_sem.at[k])
+        for k, (source, target) in enumerate([
+            (rows_hbm, rows_v), (cols_hbm, cols_v), (x_hbm, gathered.at[i]), (w_self_hbm, w_self),
+            (a_hbm, blocks.at[pl.ds(1, NBLK)]), (degree_hbm, degree_v), (w_neigh_hbm, w_neigh)])
+    ]
+    for load in loads:
+        load.start()
 
     barrier = pltpu.get_barrier_semaphore()
     near = [(0, 1, 0), (0, -1, 0), (1, 0, 0), (0, 0, 1)]
     for offset in near:
         pl.semaphore_signal(barrier, inc=1, device_id=(row_at(i, *offset), j), device_id_type=MESH)
-    for k in range(7):
-        pl.semaphore_signal(
-            barrier, inc=1, device_id=(i, col_at(j, *step_offset(k))), device_id_type=MESH)
-    pl.semaphore_wait(barrier, len(near) + 7)
+    for offset in (OVER, RIGHT, LEFT):
+        pl.semaphore_signal(barrier, inc=1, device_id=(i, col_at(j, *offset)), device_id_type=MESH)
+    pl.semaphore_wait(barrier, len(near) + 3)
 
     def gather_copy(name, arriving=False):
         _, (dz, dx), first, count, target = SENDS[name]
@@ -108,19 +135,26 @@
 
     waited = set()
 
-    def gather_steps(steps):
-        for name, copies in steps:
-            if name is not None:
-                gather_copy(name, arriving=True).wait_recv()
-                waited.add(name)
-            for copy in copies:
-                gather_copy(copy[0]).start()
-
-    gather_steps(PLAN[:1])
-
+    def gather_wait(*names):
+        for name in names:
+            gather_copy(name, arriving=True).wait_recv()
+            waited.add(name)
+
+    def gather_steps(*names):
+        for name, copies in PLAN:
+            if name in names:
+                if name is not None:
+                    gather_wait(name)
+                for copy in copies:
+                    gather_copy(copy[0]).start()
+
+    gather_steps(None)
+
+    loads[0].wait()
+    loads[1].wait()
     slots[...] = jnp.full_like(slots, -1)
-    slots[0:1, 0:NBLK] = rows_ref[...]
-    slots[1:2, 0:NBLK] = cols_ref[...]
+    slots[0:1, 0:NBLK] = rows_v[...]
+    slots[1:2, 0:NBLK] = cols_v[...]
     place = lax.broadcasted_iota(jnp.int32, (COL_BLOCKS, LANES), 1) + 1
     here = lax.broadcasted_iota(jnp.int32, (COL_BLOCKS, LANES), 0) == slots[1:2, :]
     in_row = lax.broadcasted_iota(jnp.int32, (ROW_BLOCKS, LANES), 0) == slots[0:1, :]
@@ -135,98 +169,150 @@
     table_copy.start()
     blocks[0] = jnp.zeros((BS, BS), jnp.bfloat16)
 
-    gather_steps(PLAN[1:3])
-    x_load.wait()
-    gather_steps(PLAN[3:4])
+    def clear(k, _):
+        acc[k] = jnp.zeros((PIECE, D), jnp.float32)
+        return 0
+
+    lax.fori_loop(0, 8, clear, 0)
+    loads[2].wait()
+    loads[3].wait()
     for b in range(4):
         rows = pl.ds(b * BS, BS)
         own[rows, :] = jnp.dot(
-            gathered[i, rows, :], w_self_ref[...], preferred_element_type=jnp.float32)
-    gather_steps(PLAN[4:])
+            gathered[i, rows, :], w_self[...], preferred_element_type=jnp.float32)
+    gather_steps("a1", "a2", "bz", "b1", "b2", "az")
     table_copy.wait()
-    for name in SENDS:
-        if name not in waited:
-            gather_copy(name, arriving=True).wait_recv()
-    load.wait()
-
-    def piece_sum(piece):
-        acc[...] = jnp.zeros_like(acc)
-
-        def chunk(c, _):
-            for p in range(0, CHUNK, 2):
-                first = c * CHUNK + p
-                block = first % 4
-                x = gathered[first // 4, pl.ds(pl.multiple_of(block * BS, 2 * BS), 2 * BS), :]
-                for b in range(4):
-                    r = piece * 4 + b
-                    a = jnp.concatenate(
-                        [blocks[table_s[r, first]], blocks[table_s[r, first + 1]]], axis=1)
-                    acc[b] += jnp.dot(a, x, preferred_element_type=jnp.float32)
-            return 0
-
-        lax.fori_loop(0, COL_BLOCKS // CHUNK, chunk, 0)
-
-    def piece_copy(k):
+    gather_wait("s0", "s1", "s2", "s4", "s5")
+    loads[4].wait()
+
+    def add_products(k, chips):
+        piece = step_piece(j, k)
+        for b in range(4):
+            total = None
+            for dz, dx in chips:
+                chip = ((i // 8 + dz) % 2) * 4 + (i // 2 + dx + 4) % 4
+                for c in range(0, 8, 2):
+                    x = gathered[2 * chip + c // 4, pl.ds((c % 4) * BS, 2 * BS), :]
+                    slot = [table_s[piece * 4 + b, chip * 8 + c + d] for d in range(2)]
+                    a = jnp.concatenate([blocks[slot[0]], blocks[slot[1]]], axis=1)
+                    term = jnp.dot(a, x, preferred_element_type=jnp.float32)
+                    total = term if total is None else total + term
+            acc[piece, pl.ds(b * BS, BS), :] += total
+
+    def part_copy(name):
+        piece, first, count, target = PARTS[name]
         return pltpu.make_async_remote_copy(
-            src_ref=sent.at[k], dst_ref=got.at[k], send_sem=c_send.at[k], recv_sem=c_recv.at[k],
-            device_id=(i, col_at(j, *step_offset(k))), device_id_type=MESH)
-
-    def send_step(k, _):
-        piece_sum(col_at(j, *step_offset(k)))
-        for b in range(4):
-            sent[k, pl.ds(b * BS, BS), :] = acc[b].astype(jnp.bfloat16)
-        piece_copy(k).start()
+            src_ref=sent.at[STEPS.index(piece), pl.ds(first, count)],
+            dst_ref=got.at[pl.ds(PART_START[name], count)],
+            send_sem=c_send.at[PART_PLACE[name]], recv_sem=c_recv.at[PART_PLACE[name]],
+            device_id=(i, col_at(j, *target)), device_id_type=MESH)
+
+    def arrived(name, first, count):
+        start = PART_START[name] + first - PARTS[name][1]
+        return got[pl.ds(start, count), :].astype(jnp.float32)
+
+    def finish(piece, terms, parts):
+        k = STEPS.index(piece)
+        for name in terms:
+            part_copy(name).wait_recv()
+        cuts = sorted({PARTS[n][1] for n in parts} | {PARTS[n][1] + PARTS[n][2] for n in parts}
+                      | {PARTS[n][1] for n in terms} | {PARTS[n][1] + PARTS[n][2] for n in terms})
+        low, high = PARTS[parts[0]][1], PARTS[parts[-1]][1] + PARTS[parts[-1]][2]
+        cuts = [c for c in cuts if low <= c <= high]
+        for first, last in zip(cuts, cuts[1:]):
+            value = acc[col_at(j, *piece), pl.ds(first, last - first), :]
+            for name in terms:
+                if PARTS[name][1] <= first and last <= PARTS[name][1] + PARTS[name][2]:
+                    value += arrived(name, first, last - first)
+            sent[k, pl.ds(first, last - first), :] = value.astype(jnp.bfloat16)
+        for name in parts:
+            part_copy(name).start()
+
+    def early_step(k, _):
+        add_products(k, EARLY)
+        for step, names in enumerate([
+                ("a3", "a4"), ("zb1", "zb2"), ("az1", "az2"), ("b3", "b4"), ("zb3", "zb4"),
+                ("az3", "az4")]):
+            @pl.when(k == step)
+            def _(names=names):
+                gather_steps(*names)
         return 0
 
-    lax.fori_loop(0, 7, send_step, 0)
-    piece_sum(j)
-    for k in range(7):
-        piece_copy(k).wait_recv()
+    lax.fori_loop(0, 8, early_step, 0)
+    gather_wait(*[name for name in SENDS if name not in waited])
+
+    actions = {
+        0: [((1, 2), [], ["z2", "o2r", "o2l"])],
+        1: [((1, -1), [], ["zl"]), ((1, -1), ["o2l"], ["o1l"])],
+        2: [((1, 1), [], ["zr"]), ((1, 1), ["o2r"], ["o1r"])],
+        4: [((0, 2), ["z2"], ["n2r", "n2l"])],
+        5: [((1, 0), ["o1r", "o1l"], ["o0"])],
+        6: [((0, -1), ["zl", "n2l"], ["n1l"])],
+        7: [((0, 1), ["zr", "n2r"], ["n1r"])],
+    }
+
+    def late_step(k, _):
+        add_products(k, LATE)
+        for step, todo in actions.items():
+            @pl.when(k == step)
+            def _(todo=todo):
+                for piece, terms, parts in todo:
+                    finish(piece, terms, parts)
+        return 0
+
+    lax.fori_loop(0, 8, late_step, 0)
+    loads[5].wait()
+    loads[6].wait()
+    for name in ("n1r", "n1l", "o0"):
+        part_copy(name).wait_recv()
     for b in range(4):
         rows = pl.ds(b * BS, BS)
-        total = acc[b]
-        for k in range(7):
-            total += got[k, rows, :].astype(jnp.float32)
-        degree = jnp.broadcast_to(degree_ref[b:b + 1, :].astype(jnp.float32), (BS, BS)).T
+        total = acc[j, rows, :]
+        for name in ("n1r", "n1l", "o0"):
+            total += arrived(name, b * BS, BS)
+        degree = jnp.broadcast_to(degree_v[b:b + 1, :].astype(jnp.float32), (BS, BS)).T
         degree = jnp.concatenate([degree, degree], axis=1)
         mean = (total / degree).astype(jnp.bfloat16)
-        new = own[rows, :] + jnp.dot(mean, w_neigh_ref[...], preferred_element_type=jnp.float32)
+        new = own[rows, :] + jnp.dot(mean, w_neigh[...], preferred_element_type=jnp.float32)
         out_ref[rows, :] = jnp.maximum(new, 0.0).astype(jnp.bfloat16)
-    for k in range(7):
-        piece_copy(k).wait_send()
+    for name in PARTS:
+        part_copy(name).wait_send()
     for name in SENDS:
         gather_copy(name).wait_send()
 
 
 def per_device(features, weights, slot_row, slot_column, degree, w_self, w_neigh):
-    vmem = pl.BlockSpec(memory_space=pltpu.VMEM)
-    hbm = pl.BlockSpec(memory_space=pl.ANY)
+    hbm = pl.BlockSpec(memory_space=pltpu.HBM)
     count = len(SENDS)
     return pl.pallas_call(
         kernel,
         out_shape=jax.ShapeDtypeStruct((PIECE, D), jnp.bfloat16),
-        in_specs=[vmem] * 5 + [hbm] * 2,
-        out_specs=vmem,
+        in_specs=[hbm] * 7,
+        out_specs=pl.BlockSpec(memory_space=pltpu.VMEM),
         scratch_shapes=[
             pltpu.VMEM((16, PIECE, D), jnp.bfloat16),
             pltpu.VMEM((NBLK + 1, BS, BS), jnp.bfloat16),
             pltpu.VMEM((ROW_BLOCKS, COL_BLOCKS), jnp.int32),
             pltpu.SMEM((ROW_BLOCKS, COL_BLOCKS), jnp.int32),
             pltpu.VMEM((PIECE, D), jnp.float32),
-            pltpu.VMEM((4, BS, D), jnp.float32),
+            pltpu.VMEM((8, PIECE, D), jnp.float32),
             pltpu.VMEM((7, PIECE, D), jnp.bfloat16),
-            pltpu.VMEM((7, PIECE, D), jnp.bfloat16),
+            pltpu.VMEM((PART_ROWS, D), jnp.bfloat16),
             pltpu.VMEM((8, LANES), jnp.int32),
-            pltpu.SemaphoreType.DMA,
-            pltpu.SemaphoreType.DMA,
+            pltpu.VMEM((1, NBLK), jnp.int32),
+            pltpu.VMEM((1, NBLK), jnp.int32),
+            pltpu.VMEM((4, BS), jnp.int32),
+            pltpu.VMEM((D, D), jnp.bfloat16),
+            pltpu.VMEM((D, D), jnp.bfloat16),
+            pltpu.SemaphoreType.DMA((7,)),
             pltpu.SemaphoreType.DMA,
             pltpu.SemaphoreType.DMA((count,)),
             pltpu.SemaphoreType.DMA((count,)),
-            pltpu.SemaphoreType.DMA((7,)),
-            pltpu.SemaphoreType.DMA((7,)),
+            pltpu.SemaphoreType.DMA((len(PARTS),)),
+            pltpu.SemaphoreType.DMA((len(PARTS),)),
         ],
         compiler_params=pltpu.CompilerParams(
-            collective_id=0, has_side_effects=True, vmem_limit_bytes=52 * 2**20),
+            collective_id=0, has_side_effects=True, vmem_limit_bytes=60 * 2**20),
         name="sage_layer",
     )(
         slot_row.reshape(1, NBLK), slot_column.reshape(1, NBLK), degree.reshape(4, BS),

time: 65.1 us -> 52.2 us (0.80); the launches traced: 63.8 us -> 52.1 us
  Pallas kernels: 58.3 us -> 50.4 us
  local copies, waits for them, and re-layouts: 5.51 us -> 1.67 us
    pallas_call x1, Pallas kernels: 58.3 us -> 50.4 us  [per_device(): pl.pallas_call(kernel, out_shape=jax.ShapeDtypeStruct((PIECE, D), jnp.bfl...]
    unnamed x13 -> x1, local copies, waits for them, and re-layouts: 5.51 us -> 1.67 us
where the time goes in v2:
time: 52.2 us; the launch traced here: 52.1 us
  Pallas kernels  50.4 us (97%)
  local copies, waits for them, and re-layouts  1.67 us (3%)
    pallas_call x1, Pallas kernels, per_device(): pl.pallas_call(kernel, out_shape=jax.ShapeDtypeStruct((PIECE, D), jnp.bfl...  50.4 us
    unnamed x1, local copies, waits for them, and re-layouts  1.67 us

profile of v2, /device:TPU:0, one launch (start us, length us, event | category | flops | bytes accessed | tf_op | source)
XLA Modules:
  0.0 52.1 jit_solution(17011427117253935705)
XLA Ops:
  0.0 50.4 %sage_layer.1 = bf16[512,256]{1,0:T(8,128)(2,1)} custom-call(s32[1,736]{1,0:T(1,128)} %bitcast.5, s32[1,736]{1,0:T(1,128)} %bitcast.6, s32[4,128]{1,0:T(4,128)} %bitcast.7, bf16[256,256]{1,0:T(8,128)(2,1)} %w_self_hbm.1, bf16[256,256]{1,0:T(8,128)(2,1)} %w_neigh_hbm.1, bf16[512,256]{1,0:T(8,128)(2,1)} %x_hbm.1, bf16[736,128,128]{2,1,0:T(8,128)(2,1)} %bitcast.4), custom_call_target="tpu_custom_call" | custom-call | tf_op jit(solution)/shard_map/sage_layer/pallas_call | solution.py:287
  50.4 1.7 %copy.9 = bf16[512,256]{1,0:T(8,128)(2,1)} copy(bf16[512,256]{1,0:T(8,128)(2,1)} %sage_layer.1) | data formatting | bytes 524288

commit v3 on v2

v3 whole, which is shorter than its diff:
```python
import jax
import jax.numpy as jnp
from jax import lax
from jax.experimental import pallas as pl
from jax.experimental.pallas import tpu as pltpu
from jax.sharding import PartitionSpec as P

MESH = pl.DeviceIdType.MESH
BS = 128
D = 256
PIECE = 512
NBLK = 736
LANES = 768
ROW_BLOCKS = 32
COL_BLOCKS = 64
UPPER = 224


def row_at(i, dz, dx, dc):
    return ((i // 8 + dz) % 2) * 8 + ((i // 2 + dx + 4) % 4) * 2 + (i + dc) % 2


def col_at(j, dz, dy):
    return ((j // 4 + dz) % 2) * 4 + (j + dy + 4) % 4


def gather_plan():
    upper, lower = (0, UPPER), (UPPER, PIECE - UPPER)
    first, second = (0, UPPER // 2), (UPPER // 2, UPPER // 2)
    rest = (PIECE - UPPER) // 2
    third, fourth = (UPPER, rest), (UPPER + rest, rest)
    right, left, over, core = (0, 1, 0), (0, -1, 0), (1, 0, 0), (0, 0, 1)
    return [
        (None, [
            ("a1", (0, 0), *upper, right), ("a2", (0, 0), *upper, left),
            ("bz", (0, 0), *lower, over), ("az", (0, 0), *upper, over),
            ("b1", (0, 0), *lower, right), ("b2", (0, 0), *lower, left),
            ("s0", (0, 0), 0, PIECE, core)]),
        ("a1", [("az1", (0, -1), *upper, over), ("a3", (0, -1), *first, right),
                ("s1", (0, -1), *upper, core)]),
        ("a2", [("az2", (0, 1), *upper, over), ("a4", (0, 1), *second, left),
                ("s2", (0, 1), *upper, core)]),
        ("bz", [("zb1", (1, 0), *lower, right), ("zb2", (1, 0), *lower, left),
                ("s3", (1, 0), *lower, core)]),
        ("b1", [("b3", (0, -1), *third, right), ("s4", (0, -1), *lower, core)]),
        ("b2", [("b4", (0, 1), *fourth, left), ("s5", (0, 1), *lower, core)]),
        ("az", [("s6", (1, 0), *upper, core)]),
        ("a3", [("az3", (0, 2), *first, over), ("s7", (0, 2), *first, core)]),
        ("a4", [("az4", (0, 2), *second, over), ("s8", (0, 2), *second, core)]),
        ("zb1", [("zb3", (1, -1), *third, right), ("s9", (1, -1), *lower, core)]),
        ("zb2", [("zb4", (1, 1), *fourth, left), ("s10", (1, 1), *lower, core)]),
        ("az1", [("s11", (1, -1), *upper, core)]),
        ("az2", [("s12", (1, 1), *upper, core)]),
        ("b3", [("s13", (0, 2), *third, core)]),
        ("b4", [("s14", (0, 2), *fourth, core)]),
        ("zb3", [("s15", (1, 2), *third, core)]),
        ("zb4", [("s16", (1, 2), *fourth, core)]),
        ("az3", [("s17", (1, 2), *first, core)]),
        ("az4", [("s18", (1, 2), *second, core)]),
    ]


PLAN = gather_plan()
SENDS = {copy[0]: copy for _, copies in PLAN for copy in copies}
PLACE = {name: k for k, name in enumerate(SENDS)}
PASSED_ON = [name for name, _ in PLAN]


PIECES = [(1, 2), (0, 2), (1, -1), (1, 1), (0, -1), (0, 1), (1, 0), (0, 0)]
WHOLE = [(piece, 0) for piece in PIECES]
HALVES = [
    ((1, 2), 0), ((1, 2), 2), ((0, 2), 2), ((1, -1), 0), ((1, -1), 2), ((1, 1), 0), ((1, 1), 2),
    ((0, 2), 0), ((1, 0), 0), ((0, -1), 2), ((0, 1), 2), ((1, 0), 2), ((0, -1), 0), ((0, 1), 0),
    ((0, 0), 0), ((0, 0), 2),
]
PROGRAM = [
    ([], WHOLE[:1], 4, {0: ("a1", "a2", "bz", "b1", "b2", "az")}),
    ([(0, 0), (0, 1), (0, -1)], WHOLE, 4, {
        0: ("a3", "a4"), 1: ("zb1", "zb2"), 2: ("az1", "az2"), 3: ("b3", "b4"),
        4: ("zb3", "zb4"), 5: ("az3", "az4")}),
    ([(1, 0), (0, 2), (1, 1), (1, -1), (1, 2)], HALVES, 2, {
        0: ("z2",), 1: ("o2r", "o2l"), 2: ("m2r", "m2l"), 3: ("zl",), 4: ("o1l",), 5: ("zr",),
        6: ("o1r",), 7: ("n2r", "n2l"), 8: ("o0z",), 9: ("m1l",), 10: ("m1r",), 11: ("o0y",),
        12: ("n1l",), 13: ("n1r",)}),
]
ZR, ZL, YL, YR = 0, 128, 256, 384
Z, Y, ALL = (ZR, YL), (YL, PIECE), (ZR, PIECE)
OVER, RIGHT, LEFT = (1, 0), (0, 1), (0, -1)
PARTS = {
    "z2": ((1, 2), Z, OVER, ()), "zl": ((1, -1), Z, OVER, ()), "zr": ((1, 1), Z, OVER, ()),
    "o2r": ((1, 2), (YR, PIECE), RIGHT, ()), "o2l": ((1, 2), (YL, YR), LEFT, ()),
    "o1r": ((1, 1), Y, RIGHT, ("o2r",)), "o1l": ((1, -1), Y, LEFT, ("o2l",)),
    "n2r": ((0, 2), (ZR, ZL), RIGHT, ("z2",)), "n2l": ((0, 2), (ZL, YL), LEFT, ("z2",)),
    "m2r": ((0, 2), (YR, PIECE), RIGHT, ()), "m2l": ((0, 2), (YL, YR), LEFT, ()),
    "n1r": ((0, 1), Z, RIGHT, ("zr", "n2r")), "n1l": ((0, -1), Z, LEFT, ("zl", "n2l")),
    "m1r": ((0, 1), Y, RIGHT, ("m2r",)), "m1l": ((0, -1), Y, LEFT, ("m2l",)),
    "o0z": ((1, 0), Z, OVER, ()), "o0y": ((1, 0), Y, OVER, ("o1r", "o1l")),
}
PART_PLACE = {name: k for k, name in enumerate(PARTS)}
PART_START = {}
PART_ROWS = 0
for _name, _part in PARTS.items():
    PART_START[_name] = PART_ROWS
    PART_ROWS += _part[1][1] - _part[1][0]


def kernel(
    rows_hbm, cols_hbm, degree_hbm, w_self_hbm, w_neigh_hbm, x_hbm, a_hbm, out_ref,
    gathered, blocks, table_v, table_s, own, acc, sent, got, slots,
    rows_v, cols_v, degree_v, shares, w_self, w_neigh,
    load_sem, table_sem, g_send, g_recv, c_send, c_recv,
):
    i, j = lax.axis_index("row"), lax.axis_index("col")

    loads = [
        pltpu.make_async_copy(source, target, load_sem.at[k])
        for k, (source, target) in enumerate([
            (rows_hbm, rows_v), (cols_hbm, cols_v), (x_hbm, gathered.at[i]), (w_self_hbm, w_self),
            (a_hbm, blocks.at[pl.ds(1, NBLK)]), (degree_hbm, degree_v), (w_neigh_hbm, w_neigh)])
    ]
    for load in loads:
        load.start()

    barrier = pltpu.get_barrier_semaphore()
    near = [(0, 1, 0), (0, -1, 0), (1, 0, 0), (0, 0, 1)]
    for offset in near:
        pl.semaphore_signal(barrier, inc=1, device_id=(row_at(i, *offset), j), device_id_type=MESH)
    for offset in (OVER, RIGHT, LEFT):
        pl.semaphore_signal(barrier, inc=1, device_id=(i, col_at(j, *offset)), device_id_type=MESH)
    pl.semaphore_wait(barrier, len(near) + 3)

    def gather_copy(name, arriving=False):
        _, (dz, dx), first, count, target = SENDS[name]
        if arriving:
            place = row_at(i, dz - target[0], dx - target[1], -target[2])
        else:
            place = row_at(i, dz, dx, 0)
        region = gathered.at[place, pl.ds(first, count)]
        source = region
        if not arriving and (dz, dx) == (0, 0):
            source = x_hbm.at[pl.ds(first, count)]
        return pltpu.make_async_remote_copy(
            src_ref=source, dst_ref=region,
            send_sem=g_send.at[PLACE[name]], recv_sem=g_recv.at[PLACE[name]],
            device_id=(row_at(i, *target), j), device_id_type=MESH)

    waited = set()

    def gather_wait(*names):
        for name in names:
            gather_copy(name, arriving=True).wait_recv()
            waited.add(name)

    def gather_steps(*names):
        for name, copies in PLAN:
            if name in names:
                if name is not None:
                    gather_wait(name)
                for copy in copies:
                    gather_copy(copy[0]).start()

    gather_steps(None)

    loads[0].wait()
    loads[1].wait()
    slots[...] = jnp.full_like(slots, -1)
    slots[0:1, 0:NBLK] = rows_v[...]
    slots[1:2, 0:NBLK] = cols_v[...]
    place = lax.broadcasted_iota(jnp.int32, (COL_BLOCKS, LANES), 1) + 1
    here = lax.broadcasted_iota(jnp.int32, (COL_BLOCKS, LANES), 0) == slots[1:2, :]
    in_row = lax.broadcasted_iota(jnp.int32, (ROW_BLOCKS, LANES), 0) == slots[0:1, :]
    in_row = in_row.astype(jnp.float32).astype(jnp.bfloat16)
    high = jnp.where(here, place >> 5, 0).astype(jnp.float32).astype(jnp.bfloat16)
    low = jnp.where(here, place & 31, 0).astype(jnp.float32).astype(jnp.bfloat16)
    dims = (((1,), (1,)), ((), ()))
    found = 32.0 * lax.dot_general(in_row, high, dims, preferred_element_type=jnp.float32)
    found += lax.dot_general(in_row, low, dims, preferred_element_type=jnp.float32)
    table_v[...] = jnp.clip(found.astype(jnp.int32), 0, NBLK)
    table_copy = pltpu.make_async_copy(table_v, table_s, table_sem)
    table_copy.start()
    blocks[0] = jnp.zeros((BS, BS), jnp.bfloat16)

    def clear(k, _):
        acc[k] = jnp.zeros((PIECE, D), jnp.float32)
        return 0

    lax.fori_loop(0, 8, clear, 0)
    loads[2].wait()
    loads[3].wait()
    for b in range(4):
        rows = pl.ds(b * BS, BS)
        own[rows, :] = jnp.dot(
            gathered[i, rows, :], w_self[...], preferred_element_type=jnp.float32)
    loads[5].wait()
    for b in range(4):
        degree = jnp.broadcast_to(degree_v[b:b + 1, :].astype(jnp.float32), (BS, BS)).T
        shares[b] = 1.0 / degree
    table_copy.wait()
    loads[4].wait()

    def add_products(piece, first, count, chips):
        for b in range(count):
            total = None
            for dz, dx in chips:
                chip = ((i // 8 + dz) % 2) * 4 + (i // 2 + dx + 4) % 4
                for c in range(0, 8, 2):
                    x = gathered[2 * chip + c // 4, pl.ds((c % 4) * BS, 2 * BS), :]
                    slot = [table_s[piece * 4 + first + b, chip * 8 + c + d] for d in range(2)]
                    a = jnp.concatenate([blocks[slot[0]], blocks[slot[1]]], axis=1)
                    term = jnp.dot(a, x, preferred_element_type=jnp.float32)
                    total = term if total is None else total + term
            acc[piece, pl.ds((first + b) * BS, BS), :] += total

    def part_copy(name):
        piece, (first, last), target, _ = PARTS[name]
        return pltpu.make_async_remote_copy(
            src_ref=sent.at[PIECES.index(piece), pl.ds(first, last - first)],
            dst_ref=got.at[pl.ds(PART_START[name], last - first)],
            send_sem=c_send.at[PART_PLACE[name]], recv_sem=c_recv.at[PART_PLACE[name]],
            device_id=(i, col_at(j, *target)), device_id_type=MESH)

    arrived = set()

    def add_arrived(value, names, first, last):
        for name in names:
            start, stop = PARTS[name][1]
            if start <= first and last <= stop:
                place = PART_START[name] + first - start
                value += got[pl.ds(place, last - first), :].astype(jnp.float32)
        return value

    def send_part(name):
        piece, (first, last), _, needs = PARTS[name]
        for need in needs:
            if need not in arrived:
                part_copy(need).wait_recv()
                arrived.add(need)
        cuts = {first, last}
        for need in needs:
            cuts |= {cut for cut in PARTS[need][1] if first < cut < last}
        cuts = sorted(cuts)
        for low, high in zip(cuts, cuts[1:]):
            value = acc[col_at(j, *piece), pl.ds(low, high - low), :]
            value = add_arrived(value, needs, low, high)
            sent[PIECES.index(piece), pl.ds(low, high - low), :] = value.astype(jnp.bfloat16)
        part_copy(name).start()

    def await_features(chip):
        for name, (_, (dz, dx), _, _, target) in SENDS.items():
            if ((dz - target[0]) % 2, (dx - target[1]) % 4) == (chip[0] % 2, chip[1] % 4):
                if name in waited:
                    continue
                gather_steps(name) if name in PASSED_ON else gather_wait(name)

    for chips, steps, count, actions in PROGRAM:
        for chip in chips:
            await_features(chip)

        for k, ((z, y), first) in enumerate(steps):
            if chips:
                add_products(col_at(j, z, y), first, count, chips)
            for name in actions.get(k, ()):
                send_part(name) if name in PARTS else gather_steps(name)

    loads[6].wait()
    for names, blocks_done in ((("m1l", "m1r", "o0y"), (2, 3)), (("o0z", "n1l", "n1r"), (0, 1))):
        for name in names:
            part_copy(name).wait_recv()
        for b in blocks_done:
            rows = pl.ds(b * BS, BS)
            total = add_arrived(acc[j, rows, :], names, b * BS, (b + 1) * BS)
            share = jnp.concatenate([shares[b], shares[b]], axis=1)
            mean = (total * share).astype(jnp.bfloat16)
            new = own[rows, :] + jnp.dot(mean, w_neigh[...], preferred_element_type=jnp.float32)
            out_ref[rows, :] = jnp.maximum(new, 0.0).astype(jnp.bfloat16)
    for name in PARTS:
        part_copy(name).wait_send()
    for name in SENDS:
        gather_copy(name).wait_send()


def per_device(features, weights, slot_row, slot_column, degree, w_self, w_neigh):
    hbm = pl.BlockSpec(memory_space=pltpu.HBM)
    count = len(SENDS)
    return pl.pallas_call(
        kernel,
        out_shape=jax.ShapeDtypeStruct((PIECE, D), jnp.bfloat16),
        in_specs=[hbm] * 7,
        out_specs=pl.BlockSpec(memory_space=pltpu.VMEM),
        scratch_shapes=[
            pltpu.VMEM((16, PIECE, D), jnp.bfloat16),
            pltpu.VMEM((NBLK + 1, BS, BS), jnp.bfloat16),
            pltpu.VMEM((ROW_BLOCKS, COL_BLOCKS), jnp.int32),
            pltpu.SMEM((ROW_BLOCKS, COL_BLOCKS), jnp.int32),
            pltpu.VMEM((PIECE, D), jnp.float32),
            pltpu.VMEM((8, PIECE, D), jnp.float32),
            pltpu.VMEM((7, PIECE, D), jnp.bfloat16),
            pltpu.VMEM((PART_ROWS, D), jnp.bfloat16),
            pltpu.VMEM((8, LANES), jnp.int32),
            pltpu.VMEM((1, NBLK), jnp.int32),
            pltpu.VMEM((1, NBLK), jnp.int32),
            pltpu.VMEM((4, BS), jnp.int32),
            pltpu.VMEM((4, BS, BS), jnp.float32),
            pltpu.VMEM((D, D), jnp.bfloat16),
            pltpu.VMEM((D, D), jnp.bfloat16),
            pltpu.SemaphoreType.DMA((7,)),
            pltpu.SemaphoreType.DMA,
            pltpu.SemaphoreType.DMA((count,)),
            pltpu.SemaphoreType.DMA((count,)),
            pltpu.SemaphoreType.DMA((len(PARTS),)),
            pltpu.SemaphoreType.DMA((len(PARTS),)),
        ],
        compiler_params=pltpu.CompilerParams(
            collective_id=0, has_side_effects=True, vmem_limit_bytes=52 * 2**20),
        name="sage_layer",
    )(*[
        pltpu.with_memory_space_constraint(operand, pltpu.HBM)
        for operand in (
            slot_row.reshape(1, NBLK), slot_column.reshape(1, NBLK), degree.reshape(4, BS),
            w_self, w_neigh, features, weights.reshape(NBLK, BS, BS))
    ])


def solution(mesh):
    in_specs = (
        P(("row", "col"), None),
        P("row", "col", None, None, None),
        P("row", "col", None),
        P("row", "col", None),
        P(("row", "col")),
        P(),
        P(),
    )
    return jax.shard_map(
        per_device, mesh=mesh, in_specs=in_specs, out_specs=P(("row", "col"), None), check_vma=False)
```

time: 52.2 us -> 45.5 us (0.87)
  Pallas kernels: 50.4 us -> 44.7 us
  local copies, waits for them, and re-layouts: 1.67 us -> 0.71 us
    pallas_call x1, Pallas kernels: 50.4 us -> 44.7 us  [per_device(): pl.pallas_call(kernel, out_shape=jax.ShapeDtypeStruct((PIECE, D), jnp.bfl...]
    unnamed x1, local copies, waits for them, and re-layouts: 1.67 us -> 0.71 us
where the time goes in v3:
time: 45.5 us; the launch traced here: 45.4 us
  Pallas kernels  44.7 us (98%)
  local copies, waits for them, and re-layouts  0.71 us (2%)
    pallas_call x1, Pallas kernels, per_device(): pl.pallas_call(kernel, out_shape=jax.ShapeDtypeStruct((PIECE, D), jnp.bfl...  44.7 us

profile of v3, /device:TPU:0, one launch (start us, length us, event | category | flops | bytes accessed | tf_op | source)
XLA Modules:
  0.0 45.4 jit_solution(4692777256134128438)
XLA Ops:
  0.0 44.7 %sage_layer.1 = bf16[512,256]{1,0:T(8,128)(2,1)S(1)} custom-call(s32[1,736]{1,0:T(1,128)} %bitcast.5, s32[1,736]{1,0:T(1,128)} %bitcast.6, s32[4,128]{1,0:T(4,128)} %bitcast.7, bf16[256,256]{1,0:T(8,128)(2,1)} %w_self_hbm.1, bf16[256,256]{1,0:T(8,128)(2,1)} %w_neigh_hbm.1, bf16[512,256]{1,0:T(8,128)(2,1)} %x_hbm.1, bf16[736,128,128]{2,1,0:T(8,128)(2,1)} %bitcast.4), custom_call_target="tpu_custom_call" | custom-call | tf_op jit(solution)/shard_map/sage_layer/pallas_call | solution.py:285
  44.7 0.7 %copy.9 = bf16[512,256]{1,0:T(8,128)(2,1)} copy(bf16[512,256]{1,0:T(8,128)(2,1)S(1)} %sage_layer.1) | data formatting | bytes 524288

commit v4 on v3

--- a/solution.py
+++ b/solution.py
@@ -75,13 +75,13 @@
 ]
 PROGRAM = [
     ([], WHOLE[:1], 4, {0: ("a1", "a2", "bz", "b1", "b2", "az")}),
-    ([(0, 0), (0, 1), (0, -1)], WHOLE, 4, {
-        0: ("a3", "a4"), 1: ("zb1", "zb2"), 2: ("az1", "az2"), 3: ("b3", "b4"),
-        4: ("zb3", "zb4"), 5: ("az3", "az4")}),
-    ([(1, 0), (0, 2), (1, 1), (1, -1), (1, 2)], HALVES, 2, {
-        0: ("z2",), 1: ("o2r", "o2l"), 2: ("m2r", "m2l"), 3: ("zl",), 4: ("o1l",), 5: ("zr",),
-        6: ("o1r",), 7: ("n2r", "n2l"), 8: ("o0z",), 9: ("m1l",), 10: ("m1r",), 11: ("o0y",),
-        12: ("n1l",), 13: ("n1r",)}),
+    ([(0, 0)], WHOLE, 4, {7: ("a3", "a4")}),
+    ([(0, 1), (0, -1)], WHOLE, 4, {
+        0: ("az1",), 2: ("zb1", "zb2"), 3: ("az2",), 4: ("b3", "b4"), 6: ("az3",),
+        7: ("zb3", "zb4", "az4")}),
+    ([(1, 0)], HALVES[:4], 2, {}),
+    ([(0, 2), (1, 1), (1, -1), (1, 2)], HALVES[:4], 2, {0: ("z2",), 1: ("o2r", "o2l"), 2: ("m2r", "m2l"), 3: ("zl",)}),
+    ([(1, 0), (0, 2), (1, 1), (1, -1), (1, 2)], HALVES[4:], 2, {1: ("zr", "o1l"), 2: ("o1r",), 3: ("n2r", "n2l"), 4: ("o0z",), 5: ("m1l",), 6: ("m1r",), 7: ("o0y",), 9: ("n1l",), 10: ("n1r",)}),
 ]
 ZR, ZL, YL, YR = 0, 128, 256, 384
 Z, Y, ALL = (ZR, YL), (YL, PIECE), (ZR, PIECE)

time: 45.5 us -> 44.9 us (0.987)
  Pallas kernels: 44.7 us -> 44.1 us
    pallas_call x1, Pallas kernels: 44.7 us -> 44.1 us  [per_device(): pl.pallas_call(kernel, out_shape=jax.ShapeDtypeStruct((PIECE, D), jnp.bfl...]
where the time goes in v4:
time: 44.9 us; the launch traced here: 44.8 us
  Pallas kernels  44.1 us (98%)
  local copies, waits for them, and re-layouts  0.71 us (2%)
    pallas_call x1, Pallas kernels, per_device(): pl.pallas_call(kernel, out_shape=jax.ShapeDtypeStruct((PIECE, D), jnp.bfl...  44.1 us

profile of v4, /device:TPU:0, one launch (start us, length us, event | category | flops | bytes accessed | tf_op | source)
XLA Modules:
  0.0 44.8 jit_solution(6083113661675322428)
XLA Ops:
  0.0 44.1 %sage_layer.1 = bf16[512,256]{1,0:T(8,128)(2,1)S(1)} custom-call(s32[1,736]{1,0:T(1,128)} %bitcast.5, s32[1,736]{1,0:T(1,128)} %bitcast.6, s32[4,128]{1,0:T(4,128)} %bitcast.7, bf16[256,256]{1,0:T(8,128)(2,1)} %w_self_hbm.1, bf16[256,256]{1,0:T(8,128)(2,1)} %w_neigh_hbm.1, bf16[512,256]{1,0:T(8,128)(2,1)} %x_hbm.1, bf16[736,128,128]{2,1,0:T(8,128)(2,1)} %bitcast.4), custom_call_target="tpu_custom_call" | custom-call | tf_op jit(solution)/shard_map/sage_layer/pallas_call | solution.py:285
  44.1 0.7 %copy.9 = bf16[512,256]{1,0:T(8,128)(2,1)} copy(bf16[512,256]{1,0:T(8,128)(2,1)S(1)} %sage_layer.1) | data formatting | bytes 524288
